TPU v7x, 128 devices: a whole 4x4x4 slice. The times are simulated.
128 devices in a mesh: gen: 8 (over y_hi, x), dom: 8 (over z, y_lo), dp: 2 (over core).
Axes of the slice: x: 4, y: 4 (y_hi: 2, y_lo: 2; y = y_hi * 2 + y_lo), z: 4, core: 2. Of those that a mesh axis runs over, the one named last changes fastest.
Arguments:
- gen_hidden: bfloat16 [2048, 4096], P(('dp', 'dom'), 'gen'), parts along dimension 0, may hold values from -52 to 52
- gen_gain: float32 [8192], P('dp'), parts along dimension 0, may hold values from 0.25 to 1.75
- gen_head: bfloat16 [131072, 4096], P(('dp', 'gen', 'dom')), parts along dimension 0, may hold values from -24 to 24
- dom_hidden: bfloat16 [2048, 4096], P(('dp', 'gen'), 'dom'), parts along dimension 0, may hold values from -52 to 52
- dom_gain: float32 [8192], P('dp'), parts along dimension 0, may hold values from 0.25 to 1.75
- dom_head: bfloat16 [131072, 4096], P(('dp', 'gen', 'dom')), parts along dimension 0, may hold values from -24 to 24
- targets: int32 [2048], P('dp'), parts along dimension 0, may hold values from 0 to 65535
- doc_ids: int32 [2048], P('dp'), parts along dimension 0, may hold values from -1 to 63, as said below
Outputs:
- token_diff: float32 [2048], P(('dp', 'dom')), parts along dimension 0
- doc_score: float32 [128], P(('dp', 'dom')), parts along dimension 0
There are 2 independent parts, one for each index of `dp`. A program takes and returns all parts, laid end to end along the dimension named above; each array names one. Nothing has to cross between parts.
Inputs may be any that keep to these rules, and one draw needn't show every extreme that they name: `doc_ids`: rows 128 * p to 128 * p + 127 form pack p. Each pack begins with rows of exactly 8 documents, numbered 8 * p onwards in order, each one row or more, and ends with padding rows marked -1. The packs fall into pairs whose document rows add up to 136, so the batch holds 544 document rows, and some pack has no padding.
All inputs are finite; a program needn't handle non-finite values.
Results may differ from a plain program's by a relative error of at most 0.0045.
Values may be sent and summed in bfloat16 or wider, within the bound.
A program may use at most 128 MiB of HBM per device.

v0:
```python
import jax
import jax.numpy as jnp
from jax import lax
from jax.sharding import PartitionSpec as P

DOC_PACK = 8


def joined(shard, axis, combine):
    everything = jax.tree.map(lambda part: lax.all_gather(part, axis), shard)
    first = jax.tree.map(lambda part: part[0], everything)

    def turn(k, so_far):
        return combine(so_far, jax.tree.map(lambda part: part[k], everything))

    return lax.fori_loop(1, lax.axis_size(axis), turn, first)


def scale_rows(values_bf, scaling, sum_axes, full_width):
    values = values_bf.astype(jnp.float32)
    meansq = jnp.sum(values * values, axis=sum_axes, keepdims=True) / full_width
    return (values * lax.rsqrt(meansq + 1e-05) * scaling).astype(jnp.bfloat16)


def row_stats(logits, wanted):
    highest = jnp.max(logits, axis=1)
    exp_total = jnp.sum(jnp.exp(logits - highest[:, None]), axis=1)
    columns = lax.broadcasted_iota(jnp.int32, logits.shape, 1)
    picked = jnp.sum(jnp.where(columns == wanted[:, None], logits, 0.0), axis=1)
    return (highest, exp_total, picked)


def combine(former, latter):
    highest = jnp.maximum(former[0], latter[0])
    exp_total = former[1] * jnp.exp(former[0] - highest) + latter[1] * jnp.exp(latter[0] - highest)
    return (highest, exp_total, former[2] + latter[2])


def general_stats(gen_hidden, gen_gain, gen_head, wanted_all):
    rows_dev, width_dev = gen_hidden.shape
    full_width = gen_gain.shape[0]
    gen_count = lax.axis_size("gen")
    dom_count = lax.axis_size("dom")
    block_rows = gen_head.shape[0]
    rows_all = rows_dev * dom_count
    blocks = lax.all_gather(gen_hidden[None], ("gen", "dom"), axis=0, tiled=True)
    blocks = blocks.reshape(gen_count, rows_all, width_dev)
    gain_blocks = gen_gain.reshape(gen_count, 1, width_dev)
    head_blocks = gen_head.reshape(block_rows, gen_count, width_dev)
    normed = scale_rows(blocks, gain_blocks, (0, 2), full_width)
    logits = lax.dot_general(
        normed, head_blocks, (((0, 2), (1, 2)), ((), ())), preferred_element_type=jnp.float32
    )
    row_totals = row_stats(logits, wanted_all)
    highest, exp_total, picked = joined(row_totals, ("gen", "dom"), combine)
    return picked - (highest + jnp.log(exp_total))


def domain_stats(dom_hidden, dom_gain, dom_head, wanted_all):
    rows_dev, width_dev = dom_hidden.shape
    full_width = dom_gain.shape[0]
    gen_count = lax.axis_size("gen")
    dom_count = lax.axis_size("dom")
    block_rows = dom_head.shape[0]
    rows_all = rows_dev * gen_count
    blocks = lax.all_gather(dom_hidden[None], ("gen", "dom"), axis=0, tiled=True)
    blocks = blocks.reshape(gen_count, dom_count, rows_dev, width_dev)
    head_blocks = dom_head.reshape(block_rows, dom_count, width_dev)
    gain_blocks = dom_gain.reshape(1, dom_count, 1, width_dev)
    normed = scale_rows(blocks, gain_blocks, (1, 3), full_width)
    logits = lax.dot_general(
        normed, head_blocks, (((1, 3), (1, 2)), ((), ())), preferred_element_type=jnp.float32
    )
    row_totals = row_stats(logits.reshape(rows_all, block_rows), wanted_all)
    highest, exp_total, picked = joined(row_totals, ("gen", "dom"), combine)
    return picked - (highest + jnp.log(exp_total))


def per_device(gen_hidden, gen_gain, gen_head, dom_hidden, dom_gain, dom_head, targets, doc_ids):
    rows_dev = gen_hidden.shape[0]
    first_column = (
        lax.axis_index("gen") * lax.axis_size("dom") + lax.axis_index("dom")
    ) * gen_head.shape[0]
    wanted_all = targets - first_column
    gen_logprob = general_stats(gen_hidden, gen_gain, gen_head, wanted_all)
    dom_logprob = domain_stats(dom_hidden, dom_gain, dom_head, wanted_all)
    is_live = doc_ids >= 0
    token_all = jnp.where(is_live, dom_logprob - gen_logprob, 0.0)
    pack_index = lax.axis_index("dom")
    token_own = lax.dynamic_slice_in_dim(token_all, pack_index * rows_dev, rows_dev)
    docs_own = (
        lax.dynamic_slice_in_dim(doc_ids, pack_index * rows_dev, rows_dev) - pack_index * DOC_PACK
    )
    onehot = (docs_own[:, None] == jnp.arange(DOC_PACK, dtype=jnp.int32)[None, :]).astype(
        jnp.float32
    )
    doc_sums = jnp.dot(token_own, onehot, precision=lax.Precision.HIGHEST)
    counts = jnp.sum(onehot, axis=0)
    return (token_own, doc_sums / counts)


def solution(mesh):
    in_specs = (
        P(("dp", "dom"), "gen"),
        P("dp"),
        P(("dp", "gen", "dom"), None),
        P(("dp", "gen"), "dom"),
        P("dp"),
        P(("dp", "gen", "dom"), None),
        P("dp"),
        P("dp"),
    )
    out_specs = (P(("dp", "dom")), P(("dp", "dom")))
    return jax.shard_map(
        per_device, mesh=mesh, in_specs=in_specs, out_specs=out_specs, check_vma=False
    )
```

profile of v0, /device:TPU:0, one launch (start us, length us, event | category | flops | bytes accessed | tf_op | source)
XLA Modules:
  0.0 1784.2 jit_solution(5406152321257120198)
XLA Ops:
  7.2 0.0 all-gather.11.cloned.1.call-start
  7.2 0.7 all-gather.11.cloned.1.call-update
  7.9 0.0 all-gather.13.cloned.1.call-start
  7.9 0.7 all-gather.13.cloned.1.call-update
  8.7 0.7 mul.110
  9.4 0.7 mul.120
  10.1 0.8 dynamic-slice_subtract_fusion
  10.9 0.1 convert_reduce_fusion
  11.0 0.7 broadcast_subtract_fusion
  11.7 343.4 %all-gather.11.cloned.1.call-done = bf16[8192,512]{1,0:T(8,128)(2,1)} async-done(((bf16[128,512]{1,0:T(8,128)(2,1)}), bf16[8192,512]{1,0:T(8,128)(2,1)}) %all-gather.11.cloned.1.call-update) | async-done | bytes 8388624 | tf_op jit(solution)/shard_map/all_gather | solution.py:66
  355.0 5.1 multiply_reduce_fusion
  360.2 9.4 fusion.3
  369.5 7.6 copy.16
  377.1 321.6 %all-gather.13.cloned.1.call-done = bf16[8192,512]{1,0:T(8,128)(2,1)} async-done(((bf16[128,512]{1,0:T(8,128)(2,1)}), bf16[8192,512]{1,0:T(8,128)(2,1)}) %all-gather.13.cloned.1.call-update) | async-done | bytes 8388624 | tf_op jit(solution)/shard_map/all_gather | solution.py:46
  698.8 5.1 fusion
  703.9 0.0 copy-start
  704.0 13.2 bitcast_reduce_fusion.1
  717.2 0.0 copy-done
  717.2 2.5 fusion.2
  719.6 11.3 bitcast_reduce_fusion
  730.9 0.0 copy-start.1
  730.9 2.0 fusion.15
  733.0 174.6 %all-gather.2 = f32[65536]{0:T(1024)S(1)} all-gather(f32[1024]{0:T(1024)S(1)} %get-tuple-element.365), channel_id=4, replica_groups=mesh['gen'=8,'dom'=8,'dp'=2] {'gen','dom'}, dimensions={0}, use_global_device_ids=true | all-gather | bytes 266240 | tf_op jit(solution)/shard_map/all_gather | solution.py:10
  907.6 170.6 %all-gather.3 = f32[65536]{0:T(1024)S(1)} all-gather(f32[1024]{0:T(1024)S(1)} %get-tuple-element.364), channel_id=5, replica_groups=mesh['gen'=8,'dom'=8,'dp'=2] {'gen','dom'}, dimensions={0}, use_global_device_ids=true | all-gather | bytes 266240 | tf_op jit(solution)/shard_map/all_gather | solution.py:10
  1078.3 172.5 %all-gather.1 = f32[65536]{0:T(1024)S(1)} all-gather(f32[1024]{0:T(1024)S(1)} %get-tuple-element.408), channel_id=3, replica_groups=mesh['gen'=8,'dom'=8,'dp'=2] {'gen','dom'}, dimensions={0}, use_global_device_ids=true | all-gather | bytes 266240 | tf_op jit(solution)/shard_map/all_gather | solution.py:10
  1250.9 170.6 %all-gather.6 = f32[65536]{0:T(1024)S(1)} all-gather(f32[1024]{0:T(1024)S(1)} %get-tuple-element.368), channel_id=8, replica_groups=mesh['gen'=8,'dom'=8,'dp'=2] {'gen','dom'}, dimensions={0}, use_global_device_ids=true | all-gather | bytes 266240 | tf_op jit(solution)/shard_map/all_gather | solution.py:10
  1421.6 172.5 %all-gather.7 = f32[65536]{0:T(1024)S(1)} all-gather(f32[1024]{0:T(1024)S(1)} %get-tuple-element.369), channel_id=9, replica_groups=mesh['gen'=8,'dom'=8,'dp'=2] {'gen','dom'}, dimensions={0}, use_global_device_ids=true | all-gather | bytes 266240 | tf_op jit(solution)/shard_map/all_gather | solution.py:10
  1594.1 170.6 %all-gather.5 = f32[65536]{0:T(1024)S(1)} all-gather(f32[1024]{0:T(1024)S(1)} %get-tuple-element.406), channel_id=7, replica_groups=mesh['gen'=8,'dom'=8,'dp'=2] {'gen','dom'}, dimensions={0}, use_global_device_ids=true | all-gather | bytes 266240 | tf_op jit(solution)/shard_map/all_gather | solution.py:10
  1764.8 5.9 while.38
  1770.7 5.9 while.39
  1776.6 0.0 copy-done.1
  1776.6 0.1 dynamic_slice.66
  1776.7 0.0 copy-start.2
  1776.7 0.6 fusion.16
  1777.4 0.0 copy-done.2
  (524 shorter events, 6.0 us)
Async XLA Ops:
  7.2 347.9 %all-gather.11.cloned.1.call-start = ((), (), s32[]{:S(2)}) async-start(), calls=%async_computation | async-start | bytes 8519680 | tf_op jit(solution)/shard_map/all_gather | solution.py:66
  7.9 690.9 %all-gather.13.cloned.1.call-start = ((), (), s32[]{:S(2)}) async-start(), calls=%async_computation.1 | async-start | bytes 8519680 | tf_op jit(solution)/shard_map/all_gather | solution.py:46
  703.9 13.2 copy-start
  730.9 1045.7 %copy-start.1 = (s32[1024]{0:T(1024)S(1)}, s32[1024]{0:T(1024)}, u32[]{:S(2)}) copy-start(s32[1024]{0:T(1024)} %param.19) | copy-start | bytes 12292
  1776.7 0.6 copy-start.2
Sparse Core Ops, SparseCore 0:
  9.6 345.3 all-gather.10
  356.7 342.0 all-gather.12
where the time goes:
time: 1780 us
  blocking collectives  1030 us (58%)
  waiting for transfers between devices  666 us (37%)
  other arithmetic  27.7 us (2%)
  matrix products  25.1 us (1%)
    all_gather x6, blocking collectives, joined(): everything = jax.tree.map(lambda part: lax.all_gather(part, axis), shard)  1030 us
    all_gather x1, waiting for transfers between devices, domain_stats(): lax.all_gather(dom_hidden[None], ('gen', 'dom'), axis=0, tiled=True)  343 us
    all_gather x1, waiting for transfers between devices, general_stats(): lax.all_gather(gen_hidden[None], ('gen', 'dom'), axis=0, tiled=True)  322 us
  transfers between devices with their start and end apart: 2, of which 2 were waited for; matrix products, arithmetic and copies ran while one was open for 1% of the time, Pallas kernels for 0%

commit v1 on v0

v1 whole, which is shorter than its diff:
```python
import jax
import jax.numpy as jnp
from jax import lax
from jax.experimental import pallas as pl
from jax.experimental.pallas import tpu as pltpu
from jax.sharding import PartitionSpec as P

MESH = pl.DeviceIdType.MESH
F32 = jnp.float32
BF16 = jnp.bfloat16

PACKS = 8
PACK_ROWS = 128
DOC_PACK = 8
WIDTH = 4096
VOCAB_DEV = 1024
LANES = 128
BLOCKS = WIDTH // LANES
LIVE_ROWS = 544
THIRD_ROWS = (192, 176, 176)
THIRD_BASE = (0, 192, 368)
THIRD_PAD = 256
AXES = ((0, 1, 2), (1, 2, 0), (2, 0, 1))
LAG = 3


def turn(q):
    return q + q // 2 - 2 * (q // 3)


def device_of(x, y, z):
    return {"gen": (y // 2) * 4 + x, "dom": z * 2 + y % 2}


def slot_of(x, y, z):
    g, d = (y // 2) * 4 + x, z * 2 + y % 2
    odd = (x + y) % 2
    return (1 - odd) * (g * 4 + z) + odd * (BLOCKS + d * 4 + g // 2)


def remote(src, dst, send_sem, recv_sem, device):
    return pltpu.make_async_remote_copy(
        src_ref=src,
        dst_ref=dst,
        send_sem=send_sem,
        recv_sem=recv_sem,
        device_id=device,
        device_id_type=MESH,
    )


def kernel(
    gen_hidden,
    gen_gain,
    gen_head,
    dom_hidden,
    dom_gain,
    dom_head,
    targets,
    doc_ids,
    token_out,
    score_out,
    heads,
    x0,
    x1,
    x2,
    logits,
    place,
    normed,
    stage,
    hidden,
    gains,
    ids,
    square_in,
    square_full,
    square_src,
    square_src_full,
    stats_src,
    stats_in,
    total_src,
    total_in,
    want,
    load_sem,
    head_sem,
    stage_send,
    stage_recv,
    local_sem,
    square_send,
    square_recv,
    full_send,
    full_recv,
    full_local,
    ring_send,
    ring_recv,
    stats_send,
    stats_recv,
    total_send,
    total_recv,
):
    thirds = (x0, x1, x2)
    g, d = lax.axis_index("gen"), lax.axis_index("dom")
    core = lax.axis_index("dp")
    sign = 1 - 2 * core
    x, y, z = g % 4, (g // 4) * 2 + d % 2, d // 2
    here = (x, y, z)
    own_slot = slot_of(x, y, z)
    is_dom = (x + y) % 2
    own_block = own_slot % BLOCKS

    loads = [
        pltpu.make_async_copy(gen_hidden, hidden.at[0], load_sem.at[0]),
        pltpu.make_async_copy(dom_hidden, hidden.at[1], load_sem.at[1]),
        pltpu.make_async_copy(gen_gain, gains.at[0], load_sem.at[2]),
        pltpu.make_async_copy(dom_gain, gains.at[1], load_sem.at[3]),
        pltpu.make_async_copy(targets, ids.at[0], load_sem.at[4]),
        pltpu.make_async_copy(doc_ids, ids.at[1], load_sem.at[5]),
    ]
    for load in loads:
        load.start()

    barrier = pltpu.get_barrier_semaphore()
    for step in range(1, PACKS):
        pl.semaphore_signal(
            barrier, inc=1, device_id={"gen": (g + step) % PACKS}, device_id_type=MESH
        )
        pl.semaphore_signal(
            barrier, inc=1, device_id={"dom": (d + step) % PACKS}, device_id_type=MESH
        )
    pl.semaphore_signal(
        barrier,
        inc=1,
        device_id={"gen": (g + 4) % PACKS, "dom": d + 1 - 2 * (d % 2)},
        device_id_type=MESH,
    )
    pl.semaphore_wait(barrier, 2 * (PACKS - 1) + 1)

    gen_targets = [2 * q + g % 2 for q in range(4)]
    dom_targets = [2 * q + (d + 1) % 2 for q in range(4)]

    def stage_copy(q, model):
        cols = pl.ds(q * LANES, LANES)
        if model == 0:
            src, row, device = gen_hidden.at[:, cols], d, {"dom": gen_targets[q]}
        else:
            src, row, device = dom_hidden.at[:, cols], g, {"gen": dom_targets[q]}
        far = remote(
            src, stage.at[row], stage_send.at[model * 4 + q], stage_recv.at[row], device
        )
        near = pltpu.make_async_copy(src, stage.at[row], local_sem)
        return far, near

    def targets_self(q, model):
        return gen_targets[q] == d if model == 0 else dom_targets[q] == g

    def each_stage(act_far, act_near):
        for model in range(2):
            for q in range(4):
                mine = targets_self(q, model)
                far, near = stage_copy(q, model)
                if act_near is not None:
                    pl.when(mine)(lambda near=near: act_near(near))
                pl.when(jnp.logical_not(mine))(lambda far=far: act_far(far))

    each_stage(lambda c: c.start(), lambda c: c.start())

    loads[0].wait()
    loads[1].wait()
    for model in range(2):
        total = jnp.zeros((PACK_ROWS, LANES), F32)
        for q in range(4):
            part = hidden[model, :, q * LANES : (q + 1) * LANES].astype(F32)
            total = total + part * part
        row = jnp.sum(total.T, axis=0, keepdims=True)
        square_src[model] = row
        if model == 0:
            square_in[pl.ds(g, 1)] = row[None]
        else:
            square_in[pl.ds(PACKS + d, 1)] = row[None]

    def square_copy(step, model):
        if model == 0:
            device, own, other = {"gen": (g + step) % PACKS}, g, (g + PACKS - step) % PACKS
        else:
            device = {"dom": (d + step) % PACKS}
            own, other = PACKS + d, PACKS + (d + PACKS - step) % PACKS
        send = square_send.at[model * PACKS + step]
        out = remote(
            square_src.at[model], square_in.at[own], send, square_recv.at[own], device
        )
        arrival = remote(
            square_src.at[model], square_in.at[other], send, square_recv.at[other], device
        )
        return out, arrival

    for step in range(1, PACKS):
        for model in range(2):
            square_copy(step, model)[0].start()

    def load_heads(k, carry):
        cols = pl.ds(pl.multiple_of(k * LANES, LANES), LANES)
        pltpu.make_async_copy(gen_head.at[:, cols], heads.at[0, k], head_sem.at[0]).start()
        pltpu.make_async_copy(dom_head.at[:, cols], heads.at[1, k], head_sem.at[1]).start()
        return carry

    lax.fori_loop(0, BLOCKS, load_heads, 0)

    for step in range(1, PACKS):
        for model in range(2):
            square_copy(step, model)[1].wait_recv()
    for model in range(2):
        square_src_full[model] = jnp.sum(
            square_in[model * PACKS : (model + 1) * PACKS], axis=0
        )

    def full_copy(q, model):
        if model == 0:
            row, device = d, {"dom": gen_targets[q]}
        else:
            row, device = g, {"gen": dom_targets[q]}
        src = square_src_full.at[model]
        far = remote(src, square_full.at[row], full_send.at[model * 4 + q], full_recv.at[row], device)
        near = pltpu.make_async_copy(src, square_full.at[row], full_local)
        return far, near

    for model in range(2):
        for q in range(4):
            mine = targets_self(q, model)
            far, near = full_copy(q, model)
            pl.when(mine)(lambda near=near: near.start())
            pl.when(jnp.logical_not(mine))(lambda far=far: far.start())

    for load in loads[2:]:
        load.wait()
    docs = ids[1]
    counts = jnp.sum((docs >= 0).astype(jnp.int32), axis=1, keepdims=True)
    lane = lax.broadcasted_iota(jnp.int32, (THIRD_PAD, LANES), 1)
    sub = lax.broadcasted_iota(jnp.int32, (THIRD_PAD, LANES), 0)
    offset = jnp.zeros((1, 1), jnp.int32)
    for p in range(PACKS):
        count = counts[p : p + 1, :]
        for t in range(3):
            hit = jnp.logical_and(sub + (THIRD_BASE[t] - offset) == lane, lane < count)
            hit = jnp.logical_and(hit, sub < THIRD_ROWS[t])
            place[t, :, p * LANES : (p + 1) * LANES] = jnp.where(hit, 1.0, 0.0).astype(BF16)
        offset = offset + count

    first_column = (g * PACKS + d) * VOCAB_DEV
    tgt = ids[0]
    high, low = tgt // 256, tgt % 256
    pieces = []
    for t in range(3):
        got = jnp.zeros((32, THIRD_PAD), F32)
        for p in range(PACKS):
            rows = lax.broadcasted_iota(jnp.int32, (32, LANES), 0)
            pair = jnp.where(
                rows < 16,
                jnp.broadcast_to(high[p : p + 1, :], (32, LANES)),
                jnp.broadcast_to(low[p : p + 1, :], (32, LANES)),
            )
            got = got + lax.dot_general(
                pair.astype(F32).astype(BF16),
                place[t, :, p * LANES : (p + 1) * LANES],
                (((1,), (1,)), ((), ())),
                preferred_element_type=F32,
            )
        column = (got[0:8] * 256.0 + got[16:24]).astype(jnp.int32) - first_column
        want[t] = column

    def clear(slot, carry):
        for t in range(3):
            pad = THIRD_PAD - THIRD_ROWS[t]
            thirds[t][pl.ds(slot, 1), THIRD_ROWS[t] :, :] = jnp.zeros((1, pad, LANES), BF16)
        return carry

    lax.fori_loop(0, 2 * BLOCKS, clear, 0)

    def clear_logits(i, carry):
        rows = pl.ds(pl.multiple_of(i * 64, 64), 64)
        for a in range(6):
            logits[a, rows, :] = jnp.zeros((64, THIRD_PAD), F32)
        return carry

    lax.fori_loop(0, VOCAB_DEV // 64, clear_logits, 0)

    def source(p):
        return jnp.where(is_dom == 1, g, d) == p

    for p in range(PACKS):
        mine = source(p)

        @pl.when(jnp.logical_not(mine))
        def _(p=p):
            remote(
                stage.at[p], stage.at[p], stage_send.at[0], stage_recv.at[p], {"dom": d}
            ).wait_recv()
            remote(
                square_full.at[p], square_full.at[p], full_send.at[0], full_recv.at[p], {"dom": d}
            ).wait_recv()

        @pl.when(mine)
        def _(p=p):
            pltpu.make_async_copy(stage.at[p], stage.at[p], local_sem).wait()
            pltpu.make_async_copy(square_full.at[p], square_full.at[p], full_local).wait()

    gain = gains[is_dom, pl.ds(own_block, 1), :]
    for p in range(PACKS):
        scale = lax.rsqrt(square_full[p] / WIDTH + 1e-05)
        scale = jnp.broadcast_to(scale, (PACK_ROWS, LANES)).T
        values = stage[p].astype(F32) * scale * gain
        normed[p * PACK_ROWS : (p + 1) * PACK_ROWS, :] = values.astype(BF16)
    for t in range(3):
        rows = jnp.dot(place[t], normed[...], preferred_element_type=F32).astype(BF16)
        thirds[t][pl.ds(own_slot, 1)] = rows[None]

    def moved(axis, by):
        at = list(here)
        at[axis] = (at[axis] + by + 4) % 4
        return device_of(*at)

    ahead = [moved(axis, sign) for axis in range(3)]
    behind = [moved(axis, -sign) for axis in range(3)]

    def slot_at(t, u):
        at = list(here)
        for k in range(3):
            axis = AXES[t][k]
            at[axis] = (at[axis] - sign * u[k] + 4) % 4
        return slot_of(*at)

    def piece(t, u):
        return thirds[t].at[slot_at(t, u), pl.ds(0, THIRD_ROWS[t])]

    def ring_index(t, u):
        return t * 64 + u[0] * 16 + u[1] * 4 + u[2]

    def push(t, u, k, forward):
        new = list(u)
        new[k] = new[k] + 1 if forward else 3
        device = (ahead if forward else behind)[AXES[t][k]]
        ref = piece(t, u)
        remote(ref, ref, ring_send.at[t], ring_recv.at[ring_index(t, new)], device).start()

    def arrived(t, u):
        ref = piece(t, u)
        remote(ref, ref, ring_send.at[t], ring_recv.at[ring_index(t, u)], ahead[0]).wait_recv()

    for k in range(3):
        for t in range(3):
            push(t, (0, 0, 0), k, True)
            push(t, (0, 0, 0), k, False)
    for first in (1, 3, 2):
        for t in range(3):
            u = (first, 0, 0)
            arrived(t, u)
            if first == 1:
                push(t, u, 0, True)
            for k in (1, 2):
                push(t, u, k, True)
                push(t, u, k, False)
    for second in (1, 3, 2):

        def middle(i, carry, second=second):
            for t in range(3):
                u = (turn(i), second, 0)
                arrived(t, u)
                if second == 1:
                    push(t, u, 1, True)
                push(t, u, 2, True)
                push(t, u, 2, False)
            return carry

        lax.fori_loop(0, 4, middle, 0)

    def relay(n):
        for t in range(3):
            u = (turn(n % 4), turn(n // 4), 1)
            arrived(t, u)
            push(t, u, 2, True)

    def gather_slots(t, n):
        return [slot_at(t, (turn(n % 4), turn(n // 4), u)) for u in range(4)]

    def multiply(t, slots):
        model = slots[0] // BLOCKS
        left = jnp.concatenate([heads[model, s % BLOCKS] for s in slots], axis=1)
        right = jnp.concatenate([thirds[t][s] for s in slots], axis=1)
        return model, lax.dot_general(
            left, right, (((1,), (1,)), ((), ())), preferred_element_type=F32
        )

    def add_line(n):
        for t in range(3):
            for last in (3, 2):
                arrived(t, (turn(n % 4), turn(n // 4), last))
            s = gather_slots(t, n)
            groups = [s] if AXES[t][2] == 2 else [[s[0], s[2]], [s[1], s[3]]]
            for group in groups:
                model, product = multiply(t, group)
                logits[2 * t + model] += product

    pltpu.make_async_copy(heads.at[0], heads.at[0], head_sem.at[0]).wait()
    pltpu.make_async_copy(heads.at[1], heads.at[1], head_sem.at[1]).wait()

    def lead(n, carry):
        relay(n)
        return carry

    def steady(n, carry):
        relay(n + LAG)
        add_line(n)
        return carry

    def drain(n, carry):
        add_line(n)
        return carry

    lax.fori_loop(0, LAG, lead, 0)
    lax.fori_loop(0, 16 - LAG, steady, 0)
    lax.fori_loop(16 - LAG, 16, drain, 0)

    CHUNK = 64
    steps = VOCAB_DEV // CHUNK
    spread = jnp.zeros((32, VOCAB_DEV), F32)
    for t in range(3):

        def highest(i, so_far, t=t):
            rows = pl.ds(pl.multiple_of(i * CHUNK, CHUNK), CHUNK)
            out = []
            for model in range(2):
                block = logits[2 * t + model, rows, :].reshape(CHUNK // 8, 8, THIRD_PAD)
                out.append(jnp.maximum(so_far[model], jnp.max(block, axis=0)))
            return tuple(out)

        least = jnp.full((8, THIRD_PAD), -jnp.inf, F32)
        tops = lax.fori_loop(0, steps, highest, (least, least))
        tops = [jnp.max(top, axis=0, keepdims=True) for top in tops]
        wanted = want[t]

        def totals(i, so_far, t=t, tops=tops, wanted=wanted):
            rows = pl.ds(pl.multiple_of(i * CHUNK, CHUNK), CHUNK)
            gen = logits[2 * t, rows, :].reshape(CHUNK // 8, 8, THIRD_PAD)
            dom = logits[2 * t + 1, rows, :].reshape(CHUNK // 8, 8, THIRD_PAD)
            gen_sum = so_far[0] + jnp.sum(jnp.exp(gen - tops[0][None]), axis=0)
            dom_sum = so_far[1] + jnp.sum(jnp.exp(dom - tops[1][None]), axis=0)
            entry = (
                lax.broadcasted_iota(jnp.int32, (CHUNK // 8, 8, THIRD_PAD), 0) * 8
                + lax.broadcasted_iota(jnp.int32, (CHUNK // 8, 8, THIRD_PAD), 1)
                + i * CHUNK
            )
            picked = so_far[2] + jnp.sum(
                jnp.where(entry == wanted[None], dom - gen, 0.0), axis=0
            )
            return gen_sum, dom_sum, picked

        zero = jnp.zeros((8, THIRD_PAD), F32)
        sums = lax.fori_loop(0, steps, totals, (zero, zero, zero))
        sums = [jnp.sum(value, axis=0, keepdims=True) for value in sums]
        values = [tops[0] + jnp.log(sums[0]), tops[1] + jnp.log(sums[1]), sums[2]]
        row = lax.broadcasted_iota(jnp.int32, (32, THIRD_PAD), 0)
        stack = jnp.zeros((32, THIRD_PAD), F32)
        for k in range(3):
            rest = values[k]
            for part in range(3):
                head = rest.astype(BF16).astype(F32)
                stack = jnp.where(row == part * 8 + k, head, stack)
                rest = rest - head
        spread = spread + jnp.dot(stack.astype(BF16), place[t], preferred_element_type=F32)
    spread = spread[0:8] + spread[8:16] + spread[16:24]
    for p in range(PACKS):
        stats_src[p] = spread[:, p * LANES : (p + 1) * LANES]

    def combine(block):
        top = jnp.max(block, axis=0)
        total = top + jnp.log(jnp.sum(jnp.exp(block - top[None]), axis=0))
        row = lax.broadcasted_iota(jnp.int32, (8, LANES), 0)
        return jnp.where(row < 2, total, jnp.sum(block, axis=0))

    def stats_copy(step):
        to, other = (d + step) % PACKS, (d + PACKS - step) % PACKS
        out = remote(
            stats_src.at[to], stats_in.at[d], stats_send.at[step], stats_recv.at[d], {"dom": to}
        )
        arrival = remote(
            stats_src.at[to], stats_in.at[other], stats_send.at[step], stats_recv.at[other], {"dom": to}
        )
        return out, arrival

    for step in range(1, PACKS):
        stats_copy(step)[0].start()
    stats_in[pl.ds(d, 1)] = stats_src[pl.ds(d, 1)]
    for step in range(1, PACKS):
        stats_copy(step)[1].wait_recv()
    partial = combine(stats_in[...])
    total_src[...] = partial
    total_in[pl.ds(g, 1)] = partial[None]

    def total_copy(step):
        to, other = (g + step) % PACKS, (g + PACKS - step) % PACKS
        out = remote(
            total_src, total_in.at[g], total_send.at[step], total_recv.at[g], {"gen": to}
        )
        arrival = remote(
            total_src, total_in.at[other], total_send.at[step], total_recv.at[other], {"gen": to}
        )
        return out, arrival

    for step in range(1, PACKS):
        total_copy(step)[0].start()

    each_stage(lambda c: c.wait_send(), None)
    for model in range(2):
        for q in range(4):
            mine = targets_self(q, model)
            far, _ = full_copy(q, model)
            pl.when(jnp.logical_not(mine))(lambda far=far: far.wait_send())
    for step in range(1, PACKS):
        for model in range(2):
            square_copy(step, model)[0].wait_send()
        stats_copy(step)[0].wait_send()
    for t in range(3):
        ref = thirds[t].at[pl.ds(0, 63), pl.ds(0, THIRD_ROWS[t])]
        remote(ref, ref, ring_send.at[t], ring_recv.at[0], ahead[0]).wait_send()

    for step in range(1, PACKS):
        total_copy(step)[1].wait_recv()
    final = combine(total_in[...])
    token = final[2:3] - final[1:2] + final[0:1]
    own_docs = ids[1, pl.ds(d, 1), :]
    token = jnp.where(own_docs >= 0, token, 0.0)
    token_out[...] = token
    row = lax.broadcasted_iota(jnp.int32, (DOC_PACK, LANES), 0)
    col = lax.broadcasted_iota(jnp.int32, (DOC_PACK, LANES), 1)
    member = (own_docs - d * DOC_PACK) == row
    doc_sum = jnp.sum(jnp.where(member, token, 0.0), axis=1, keepdims=True)
    doc_count = jnp.sum(jnp.where(member, 1.0, 0.0), axis=1, keepdims=True)
    score = jnp.sum(jnp.where(row == col, doc_sum / doc_count, 0.0), axis=0, keepdims=True)
    score_out[...] = score[:, :DOC_PACK]

    for step in range(1, PACKS):
        total_copy(step)[0].wait_send()


def per_device(gen_hidden, gen_gain, gen_head, dom_hidden, dom_gain, dom_head, targets, doc_ids):
    anywhere = pl.BlockSpec(memory_space=pl.ANY)
    dma = pltpu.SemaphoreType.DMA
    slots = pltpu.VMEM((2 * BLOCKS, THIRD_PAD, LANES), BF16)
    token, score = pl.pallas_call(
        kernel,
        out_shape=(
            jax.ShapeDtypeStruct((1, PACK_ROWS), F32),
            jax.ShapeDtypeStruct((1, DOC_PACK), F32),
        ),
        in_specs=[anywhere] * 8,
        out_specs=(
            pl.BlockSpec(memory_space=pltpu.VMEM),
            pl.BlockSpec(memory_space=pltpu.VMEM),
        ),
        scratch_shapes=[
            pltpu.VMEM((2, BLOCKS, VOCAB_DEV, LANES), BF16),
            slots,
            slots,
            slots,
            pltpu.VMEM((6, VOCAB_DEV, THIRD_PAD), F32),
            pltpu.VMEM((3, THIRD_PAD, PACKS * PACK_ROWS), BF16),
            pltpu.VMEM((PACKS * PACK_ROWS, LANES), BF16),
            pltpu.VMEM((PACKS, PACK_ROWS, LANES), BF16),
            pltpu.VMEM((2, PACK_ROWS, 4 * LANES), BF16),
            pltpu.VMEM((2, BLOCKS, LANES), F32),
            pltpu.VMEM((2, PACKS, LANES), jnp.int32),
            pltpu.VMEM((2 * PACKS, 1, LANES), F32),
            pltpu.VMEM((PACKS, 1, LANES), F32),
            pltpu.VMEM((2, 1, LANES), F32),
            pltpu.VMEM((2, 1, LANES), F32),
            pltpu.VMEM((PACKS, 8, LANES), F32),
            pltpu.VMEM((PACKS, 8, LANES), F32),
            pltpu.VMEM((8, LANES), F32),
            pltpu.VMEM((PACKS, 8, LANES), F32),
            pltpu.VMEM((3, 8, THIRD_PAD), jnp.int32),
            dma((6,)),
            dma((2,)),
            dma((8,)),
            dma((8,)),
            dma,
            dma((16,)),
            dma((16,)),
            dma((8,)),
            dma((8,)),
            dma,
            dma((3,)),
            dma((192,)),
            dma((8,)),
            dma((8,)),
            dma((8,)),
            dma((8,)),
        ],
        compiler_params=pltpu.CompilerParams(
            collective_id=0, has_side_effects=True, vmem_limit_bytes=60 * 1024 * 1024
        ),
        cost_estimate=pl.CostEstimate(
            flops=4 * LIVE_ROWS * VOCAB_DEV * WIDTH,
            bytes_accessed=4 * VOCAB_DEV * WIDTH,
            transcendentals=2 * LIVE_ROWS * VOCAB_DEV,
        ),
    )(
        gen_hidden,
        gen_gain.reshape(BLOCKS, LANES),
        gen_head,
        dom_hidden,
        dom_gain.reshape(BLOCKS, LANES),
        dom_head,
        targets.reshape(PACKS, LANES),
        doc_ids.reshape(PACKS, LANES),
    )
    return token.reshape(PACK_ROWS), score.reshape(DOC_PACK)


def solution(mesh):
    in_specs = (
        P(("dp", "dom"), "gen"),
        P("dp"),
        P(("dp", "gen", "dom"), None),
        P(("dp", "gen"), "dom"),
        P("dp"),
        P(("dp", "gen", "dom"), None),
        P("dp"),
        P("dp"),
    )
    out_specs = (P(("dp", "dom")), P(("dp", "dom")))
    return jax.shard_map(
        per_device, mesh=mesh, in_specs=in_specs, out_specs=out_specs, check_vma=False
    )
```

time: 1780 us -> 100 us (0.06)
  blocking collectives: 1030 us -> 0 us
  waiting for transfers between devices: 666 us -> 0 us
  Pallas kernels: 0 us -> 97 us
  other arithmetic: 27.7 us -> 0 us
  matrix products: 25.1 us -> 0 us
    all_gather x6 -> x0, blocking collectives: 1030 us -> none  [joined(): everything = jax.tree.map(lambda part: lax.all_gather(part, axis), shard)]
    all_gather x2 -> x0, waiting for transfers between devices: 665 us -> none  [the longest x1 343 us: domain_stats(): lax.all_gather(dom_hidden[None], ('gen', 'dom'), axis=0, tiled=True)]
    pallas_call x0 -> x1, Pallas kernels: none -> 97 us  [per_device(): pl.pallas_call(kernel, out_shape=(jax.ShapeDtypeStruct((1, PACK_ROWS), F3...]
    dot_general x3 -> x0, matrix products: 25.1 us -> none  [the longest x1 13.2 us: domain_stats(): lax.dot_general(normed, head_blocks, (((1, 3), (1, 2)), ((), ())), prefer...]
  transfers between devices with their start and end apart: 2 -> 0, of which waited for: 2 -> 0; matrix products, arithmetic and copies ran while one was open for 1% -> 0% of each run, Pallas kernels for 0% -> 0%
where the time goes in v1:
time: 100 us; the launch traced here: 99.9 us
  Pallas kernels  97 us (97%)
  local copies, waits for them, and re-layouts  2.25 us (2%)
    pallas_call x1, Pallas kernels, per_device(): pl.pallas_call(kernel, out_shape=(jax.ShapeDtypeStruct((1, PACK_ROWS), F3...  97 us
    unnamed x2, local copies, waits for them, and re-layouts  2.25 us

profile of v1, /device:TPU:0, one launch (start us, length us, event | category | flops | bytes accessed | tf_op | source)
XLA Modules:
  0.0 99.9 jit_solution(8308967751191852160)
XLA Ops:
  0.6 97.0 %shard_map.95 = (f32[1,128]{1,0:T(1,128)}, f32[1,8]{1,0:T(1,128)}) custom-call(bf16[128,512]{1,0:T(8,128)(2,1)} %gen_hidden.1, f32[32,128]{1,0:T(8,128)} %bitcast.6, bf16[1024,4096]{1,0:T(8,128)(2,1)} %gen_head.1, bf16[128,512]{1,0:T(8,128)(2,1)} %dom_hidden.1, f32[32,128]{1,0:T(8,128)} %bitcast.7, bf16[1024,4096]{1,0:T(8,128)(2,1)} %dom_head.1, ...), custom_call_target="tpu_custom_call" | custom-call | flops 9126805504 | bytes 16777216 | tf_op jit(solution)/shard_map/pallas_call | solution.py:547
  97.6 1.1 %copy.12 = f32[128]{0:T(128)} copy(f32[128]{0:T(128)} %bitcast.11) | data formatting | bytes 1024
  98.8 1.1 %copy.13 = f32[8]{0:T(128)} copy(f32[8]{0:T(128)} %bitcast.10) | data formatting | bytes 64

commit v2 on v1

--- a/solution.py
+++ b/solution.py
@@ -21,7 +21,6 @@
 THIRD_BASE = (0, 192, 368)
 THIRD_PAD = 256
 AXES = ((0, 1, 2), (1, 2, 0), (2, 0, 1))
-LAG = 3
 
 
 def turn(q):
@@ -58,15 +57,13 @@
     dom_head,
     targets,
     doc_ids,
-    token_out,
-    score_out,
+    total_out,
     heads,
     x0,
     x1,
     x2,
     logits,
     place,
-    normed,
     stage,
     hidden,
     gains,
@@ -75,10 +72,10 @@
     square_full,
     square_src,
     square_src_full,
+    scale_parts,
+    scales,
     stats_src,
     stats_in,
-    total_src,
-    total_in,
     want,
     load_sem,
     head_sem,
@@ -89,13 +86,10 @@
     square_recv,
     full_send,
     full_recv,
-    full_local,
     ring_send,
     ring_recv,
     stats_send,
     stats_recv,
-    total_send,
-    total_recv,
 ):
     thirds = (x0, x1, x2)
     g, d = lax.axis_index("gen"), lax.axis_index("dom")
@@ -105,18 +99,6 @@
     here = (x, y, z)
     own_slot = slot_of(x, y, z)
     is_dom = (x + y) % 2
-    own_block = own_slot % BLOCKS
-
-    loads = [
-        pltpu.make_async_copy(gen_hidden, hidden.at[0], load_sem.at[0]),
-        pltpu.make_async_copy(dom_hidden, hidden.at[1], load_sem.at[1]),
-        pltpu.make_async_copy(gen_gain, gains.at[0], load_sem.at[2]),
-        pltpu.make_async_copy(dom_gain, gains.at[1], load_sem.at[3]),
-        pltpu.make_async_copy(targets, ids.at[0], load_sem.at[4]),
-        pltpu.make_async_copy(doc_ids, ids.at[1], load_sem.at[5]),
-    ]
-    for load in loads:
-        load.start()
 
     barrier = pltpu.get_barrier_semaphore()
     for step in range(1, PACKS):
@@ -132,36 +114,17 @@
         device_id={"gen": (g + 4) % PACKS, "dom": d + 1 - 2 * (d % 2)},
         device_id_type=MESH,
     )
-    pl.semaphore_wait(barrier, 2 * (PACKS - 1) + 1)
-
-    gen_targets = [2 * q + g % 2 for q in range(4)]
-    dom_targets = [2 * q + (d + 1) % 2 for q in range(4)]
-
-    def stage_copy(q, model):
-        cols = pl.ds(q * LANES, LANES)
-        if model == 0:
-            src, row, device = gen_hidden.at[:, cols], d, {"dom": gen_targets[q]}
-        else:
-            src, row, device = dom_hidden.at[:, cols], g, {"gen": dom_targets[q]}
-        far = remote(
-            src, stage.at[row], stage_send.at[model * 4 + q], stage_recv.at[row], device
-        )
-        near = pltpu.make_async_copy(src, stage.at[row], local_sem)
-        return far, near
-
-    def targets_self(q, model):
-        return gen_targets[q] == d if model == 0 else dom_targets[q] == g
-
-    def each_stage(act_far, act_near):
-        for model in range(2):
-            for q in range(4):
-                mine = targets_self(q, model)
-                far, near = stage_copy(q, model)
-                if act_near is not None:
-                    pl.when(mine)(lambda near=near: act_near(near))
-                pl.when(jnp.logical_not(mine))(lambda far=far: act_far(far))
-
-    each_stage(lambda c: c.start(), lambda c: c.start())
+
+    loads = [
+        pltpu.make_async_copy(gen_hidden, hidden.at[0], load_sem.at[0]),
+        pltpu.make_async_copy(dom_hidden, hidden.at[1], load_sem.at[1]),
+        pltpu.make_async_copy(gen_gain, gains.at[0], load_sem.at[2]),
+        pltpu.make_async_copy(dom_gain, gains.at[1], load_sem.at[3]),
+        pltpu.make_async_copy(targets, ids.at[0], load_sem.at[4]),
+        pltpu.make_async_copy(doc_ids, ids.at[1], load_sem.at[5]),
+    ]
+    for load in loads:
+        load.start()
 
     loads[0].wait()
     loads[1].wait()
@@ -176,6 +139,37 @@
             square_in[pl.ds(g, 1)] = row[None]
         else:
             square_in[pl.ds(PACKS + d, 1)] = row[None]
+
+    pl.semaphore_wait(barrier, 2 * (PACKS - 1) + 1)
+
+    gen_targets = [2 * q + g % 2 for q in range(4)]
+    dom_targets = [2 * q + (d + 1) % 2 for q in range(4)]
+
+    def stage_copy(q, model):
+        cols = pl.ds(q * LANES, LANES)
+        if model == 0:
+            src, row, device = gen_hidden.at[:, cols], d, {"dom": gen_targets[q]}
+        else:
+            src, row, device = dom_hidden.at[:, cols], g, {"gen": dom_targets[q]}
+        far = remote(
+            src, stage.at[row], stage_send.at[model * 4 + q], stage_recv.at[row], device
+        )
+        near = pltpu.make_async_copy(src, stage.at[row], local_sem)
+        return far, near
+
+    def targets_self(q, model):
+        return gen_targets[q] == d if model == 0 else dom_targets[q] == g
+
+    def each_stage(act_far, act_near):
+        for model in range(2):
+            for q in range(4):
+                mine = targets_self(q, model)
+                far, near = stage_copy(q, model)
+                if act_near is not None:
+                    pl.when(mine)(lambda near=near: act_near(near))
+                pl.when(jnp.logical_not(mine))(lambda far=far: act_far(far))
+
+    each_stage(lambda c: c.start(), lambda c: c.start())
 
     def square_copy(step, model):
         if model == 0:
@@ -208,26 +202,26 @@
         for model in range(2):
             square_copy(step, model)[1].wait_recv()
     for model in range(2):
-        square_src_full[model] = jnp.sum(
-            square_in[model * PACKS : (model + 1) * PACKS], axis=0
-        )
-
-    def full_copy(q, model):
+        row = jnp.sum(square_in[model * PACKS : (model + 1) * PACKS], axis=0)
+        square_src_full[model] = row
+        own = d if model == 0 else PACKS + g
+        square_full[pl.ds(own, 1)] = row[None]
+
+    def full_copy(step, model):
+        back = PACKS - step
         if model == 0:
-            row, device = d, {"dom": gen_targets[q]}
+            device, own, other = {"dom": (d + step) % PACKS}, d, (d + back) % PACKS
         else:
-            row, device = g, {"gen": dom_targets[q]}
-        src = square_src_full.at[model]
-        far = remote(src, square_full.at[row], full_send.at[model * 4 + q], full_recv.at[row], device)
-        near = pltpu.make_async_copy(src, square_full.at[row], full_local)
-        return far, near
-
-    for model in range(2):
-        for q in range(4):
-            mine = targets_self(q, model)
-            far, near = full_copy(q, model)
-            pl.when(mine)(lambda near=near: near.start())
-            pl.when(jnp.logical_not(mine))(lambda far=far: far.start())
+            device = {"gen": (g + step) % PACKS}
+            own, other = PACKS + g, PACKS + (g + back) % PACKS
+        src, send = square_src_full.at[model], full_send.at[model * PACKS + step]
+        out = remote(src, square_full.at[own], send, full_recv.at[own], device)
+        arrival = remote(src, square_full.at[other], send, full_recv.at[other], device)
+        return out, arrival
+
+    for step in range(1, PACKS):
+        for model in range(2):
+            full_copy(step, model)[0].start()
 
     for load in loads[2:]:
         load.wait()
@@ -293,23 +287,17 @@
             remote(
                 stage.at[p], stage.at[p], stage_send.at[0], stage_recv.at[p], {"dom": d}
             ).wait_recv()
-            remote(
-                square_full.at[p], square_full.at[p], full_send.at[0], full_recv.at[p], {"dom": d}
-            ).wait_recv()
 
         @pl.when(mine)
         def _(p=p):
             pltpu.make_async_copy(stage.at[p], stage.at[p], local_sem).wait()
-            pltpu.make_async_copy(square_full.at[p], square_full.at[p], full_local).wait()
-
-    gain = gains[is_dom, pl.ds(own_block, 1), :]
-    for p in range(PACKS):
-        scale = lax.rsqrt(square_full[p] / WIDTH + 1e-05)
-        scale = jnp.broadcast_to(scale, (PACK_ROWS, LANES)).T
-        values = stage[p].astype(F32) * scale * gain
-        normed[p * PACK_ROWS : (p + 1) * PACK_ROWS, :] = values.astype(BF16)
+
     for t in range(3):
-        rows = jnp.dot(place[t], normed[...], preferred_element_type=F32).astype(BF16)
+        rows = jnp.dot(
+            place[t],
+            stage[...].reshape(PACKS * PACK_ROWS, LANES),
+            preferred_element_type=F32,
+        ).astype(BF16)
         thirds[t][pl.ds(own_slot, 1)] = rows[None]
 
     def moved(axis, by):
@@ -348,75 +336,119 @@
         for t in range(3):
             push(t, (0, 0, 0), k, True)
             push(t, (0, 0, 0), k, False)
+
+    for step in range(1, PACKS):
+        for model in range(2):
+            full_copy(step, model)[1].wait_recv()
+    for model in range(2):
+        for p in range(PACKS):
+            rest = lax.rsqrt(square_full[model * PACKS + p] / WIDTH + 1e-05)
+            rest = jnp.broadcast_to(rest, (PACK_ROWS, LANES)).T
+            for part in range(3):
+                head = rest.astype(BF16)
+                scale_parts[part, p * PACK_ROWS : (p + 1) * PACK_ROWS, :] = head
+                rest = rest - head.astype(F32)
+        for t in range(3):
+            total = jnp.zeros((THIRD_PAD, LANES), F32)
+            for part in range(3):
+                total = total + jnp.dot(
+                    place[t], scale_parts[part], preferred_element_type=F32
+                )
+            scales[2 * t + model] = total
+
     for first in (1, 3, 2):
         for t in range(3):
             u = (first, 0, 0)
             arrived(t, u)
             if first == 1:
                 push(t, u, 0, True)
-            for k in (1, 2):
-                push(t, u, k, True)
-                push(t, u, k, False)
-    for second in (1, 3, 2):
-
-        def middle(i, carry, second=second):
-            for t in range(3):
-                u = (turn(i), second, 0)
-                arrived(t, u)
-                if second == 1:
-                    push(t, u, 1, True)
-                push(t, u, 2, True)
-                push(t, u, 2, False)
-            return carry
-
-        lax.fori_loop(0, 4, middle, 0)
-
-    def relay(n):
-        for t in range(3):
-            u = (turn(n % 4), turn(n // 4), 1)
+            push(t, u, 1, True)
+            push(t, u, 1, False)
+    for first in (1, 3, 2):
+        for t in range(3):
+            push(t, (first, 0, 0), 2, True)
+            push(t, (first, 0, 0), 2, False)
+
+    def line(n, last):
+        return turn(n % 4), turn(n // 4), last
+
+    def announce(t, n):
+        push(t, line(n, 0), 2, True)
+        push(t, line(n, 0), 2, False)
+
+    def relay(t, n):
+        arrived(t, line(n, 1))
+        push(t, line(n, 1), 2, True)
+
+    def middle(i, carry):
+        for t in range(3):
+            u = (turn(i), 1, 0)
             arrived(t, u)
+            push(t, u, 1, True)
             push(t, u, 2, True)
-
-    def gather_slots(t, n):
-        return [slot_at(t, (turn(n % 4), turn(n // 4), u)) for u in range(4)]
-
-    def multiply(t, slots):
-        model = slots[0] // BLOCKS
-        left = jnp.concatenate([heads[model, s % BLOCKS] for s in slots], axis=1)
-        right = jnp.concatenate([thirds[t][s] for s in slots], axis=1)
-        return model, lax.dot_general(
-            left, right, (((1,), (1,)), ((), ())), preferred_element_type=F32
-        )
-
-    def add_line(n):
-        for t in range(3):
-            for last in (3, 2):
-                arrived(t, (turn(n % 4), turn(n // 4), last))
-            s = gather_slots(t, n)
-            groups = [s] if AXES[t][2] == 2 else [[s[0], s[2]], [s[1], s[3]]]
-            for group in groups:
-                model, product = multiply(t, group)
-                logits[2 * t + model] += product
+            push(t, u, 2, False)
+        return carry
+
+    lax.fori_loop(0, 4, middle, 0)
+
+    def add_layer(t, half, last):
+        slots = [slot_at(t, line(8 * half + i, last)) for i in range(8)]
+        if t == 0:
+            order = (0, 3, 5, 6, 1, 2, 4, 7)
+        elif t == 1:
+            order = (0, 3, 4, 7, 1, 2, 5, 6)
+        else:
+            order = (0, 1, 2, 3, 4, 5, 6, 7)
+        for group in (order[:4], order[4:]):
+            group = [slots[i] for i in group]
+            model = group[0] // BLOCKS
+            left = jnp.concatenate([heads[model, s % BLOCKS] for s in group], axis=1)
+            scale = scales[2 * t + model]
+            right = jnp.concatenate(
+                [
+                    (
+                        thirds[t][s].astype(F32) * scale * gains[model, pl.ds(s % BLOCKS, 1), :]
+                    ).astype(BF16)
+                    for s in group
+                ],
+                axis=1,
+            )
+            logits[2 * t + model] += lax.dot_general(
+                left, right, (((1,), (1,)), ((), ())), preferred_element_type=F32
+            )
 
     pltpu.make_async_copy(heads.at[0], heads.at[0], head_sem.at[0]).wait()
     pltpu.make_async_copy(heads.at[1], heads.at[1], head_sem.at[1]).wait()
 
-    def lead(n, carry):
-        relay(n)
+    def layer(k, carry):
+        half = jnp.where((k == 3) | (k >= 5), 1, 0)
+        last = jnp.where((k == 1) | (k == 5), 3, 0)
+        last = jnp.where((k == 2) | (k == 6), 1, last)
+        last = jnp.where((k == 4) | (k == 7), 2, last)
+        for t in range(3):
+
+            @pl.when(last >= 2)
+            def _(t=t):
+                for i in range(8):
+                    arrived(t, line(8 * half + i, last))
+
+            add_layer(t, half, last)
+
+            @pl.when(k < 2)
+            def _(t=t):
+                for i in range(4):
+                    n = 8 + 4 * k + i
+                    arrived(t, line(n, 0))
+                    announce(t, n)
+
+            @pl.when((k < 2) | (k == 3) | (k == 4))
+            def _(t=t):
+                for i in range(4):
+                    relay(t, 4 * (k - k // 3) + i)
+
         return carry
 
-    def steady(n, carry):
-        relay(n + LAG)
-        add_line(n)
-        return carry
-
-    def drain(n, carry):
-        add_line(n)
-        return carry
-
-    lax.fori_loop(0, LAG, lead, 0)
-    lax.fori_loop(0, 16 - LAG, steady, 0)
-    lax.fori_loop(16 - LAG, 16, drain, 0)
+    lax.fori_loop(0, 8, layer, 0)
 
     CHUNK = 64
     steps = VOCAB_DEV // CHUNK
@@ -467,65 +499,46 @@
         spread = spread + jnp.dot(stack.astype(BF16), place[t], preferred_element_type=F32)
     spread = spread[0:8] + spread[8:16] + spread[16:24]
     for p in range(PACKS):
-        stats_src[p] = spread[:, p * LANES : (p + 1) * LANES]
-
-    def combine(block):
-        top = jnp.max(block, axis=0)
-        total = top + jnp.log(jnp.sum(jnp.exp(block - top[None]), axis=0))
-        row = lax.broadcasted_iota(jnp.int32, (8, LANES), 0)
-        return jnp.where(row < 2, total, jnp.sum(block, axis=0))
-
-    def stats_copy(step):
-        to, other = (d + step) % PACKS, (d + PACKS - step) % PACKS
-        out = remote(
-            stats_src.at[to], stats_in.at[d], stats_send.at[step], stats_recv.at[d], {"dom": to}
-        )
-        arrival = remote(
-            stats_src.at[to], stats_in.at[other], stats_send.at[step], stats_recv.at[other], {"dom": to}
-        )
-        return out, arrival
-
-    for step in range(1, PACKS):
-        stats_copy(step)[0].start()
-    stats_in[pl.ds(d, 1)] = stats_src[pl.ds(d, 1)]
-    for step in range(1, PACKS):
-        stats_copy(step)[1].wait_recv()
-    partial = combine(stats_in[...])
-    total_src[...] = partial
-    total_in[pl.ds(g, 1)] = partial[None]
-
-    def total_copy(step):
-        to, other = (g + step) % PACKS, (g + PACKS - step) % PACKS
-        out = remote(
-            total_src, total_in.at[g], total_send.at[step], total_recv.at[g], {"gen": to}
-        )
-        arrival = remote(
-            total_src, total_in.at[other], total_send.at[step], total_recv.at[other], {"gen": to}
-        )
-        return out, arrival
-
-    for step in range(1, PACKS):
-        total_copy(step)[0].start()
+        stats_src[p] = spread[0:4, p * LANES : (p + 1) * LANES]
+
+    me = g * PACKS + d
+
+    def share(step, carry):
+        peer = (me + step) % (PACKS * PACKS)
+        remote(
+            stats_src.at[peer % PACKS],
+            stats_in.at[me],
+            stats_send,
+            stats_recv,
+            {"gen": peer // PACKS, "dom": peer % PACKS},
+        ).start()
+        return carry
+
+    lax.fori_loop(1, PACKS * PACKS, share, 0)
+    stats_in[pl.ds(me, 1)] = stats_src[pl.ds(d, 1)]
 
     each_stage(lambda c: c.wait_send(), None)
-    for model in range(2):
-        for q in range(4):
-            mine = targets_self(q, model)
-            far, _ = full_copy(q, model)
-            pl.when(jnp.logical_not(mine))(lambda far=far: far.wait_send())
     for step in range(1, PACKS):
         for model in range(2):
             square_copy(step, model)[0].wait_send()
-        stats_copy(step)[0].wait_send()
+            full_copy(step, model)[0].wait_send()
     for t in range(3):
         ref = thirds[t].at[pl.ds(0, 63), pl.ds(0, THIRD_ROWS[t])]
         remote(ref, ref, ring_send.at[t], ring_recv.at[0], ahead[0]).wait_send()
 
-    for step in range(1, PACKS):
-        total_copy(step)[1].wait_recv()
-    final = combine(total_in[...])
-    token = final[2:3] - final[1:2] + final[0:1]
-    own_docs = ids[1, pl.ds(d, 1), :]
+    others = stats_in.at[pl.ds(0, PACKS * PACKS - 1)]
+    remote(others, others, stats_send, stats_recv, ahead[0]).wait()
+    block = stats_in[...]
+    top = jnp.max(block, axis=0)
+    total = top + jnp.log(jnp.sum(jnp.exp(block - top[None]), axis=0))
+    row = lax.broadcasted_iota(jnp.int32, (4, LANES), 0)
+    total_out[...] = jnp.where(row < 2, total, jnp.sum(block, axis=0))
+
+
+def finish(total, doc_ids, token_out, score_out):
+    d = lax.axis_index("dom")
+    token = total[2:3, :] - total[1:2, :] + total[0:1, :]
+    own_docs = doc_ids[pl.ds(d, 1), :]
     token = jnp.where(own_docs >= 0, token, 0.0)
     token_out[...] = token
     row = lax.broadcasted_iota(jnp.int32, (DOC_PACK, LANES), 0)
@@ -536,25 +549,17 @@
     score = jnp.sum(jnp.where(row == col, doc_sum / doc_count, 0.0), axis=0, keepdims=True)
     score_out[...] = score[:, :DOC_PACK]
 
-    for step in range(1, PACKS):
-        total_copy(step)[0].wait_send()
-
 
 def per_device(gen_hidden, gen_gain, gen_head, dom_hidden, dom_gain, dom_head, targets, doc_ids):
     anywhere = pl.BlockSpec(memory_space=pl.ANY)
     dma = pltpu.SemaphoreType.DMA
     slots = pltpu.VMEM((2 * BLOCKS, THIRD_PAD, LANES), BF16)
-    token, score = pl.pallas_call(
+    docs = doc_ids.reshape(PACKS, LANES)
+    total = pl.pallas_call(
         kernel,
-        out_shape=(
-            jax.ShapeDtypeStruct((1, PACK_ROWS), F32),
-            jax.ShapeDtypeStruct((1, DOC_PACK), F32),
-        ),
+        out_shape=jax.ShapeDtypeStruct((4, LANES), F32),
         in_specs=[anywhere] * 8,
-        out_specs=(
-            pl.BlockSpec(memory_space=pltpu.VMEM),
-            pl.BlockSpec(memory_space=pltpu.VMEM),
-        ),
+        out_specs=pl.BlockSpec(memory_space=pltpu.VMEM),
         scratch_shapes=[
             pltpu.VMEM((2, BLOCKS, VOCAB_DEV, LANES), BF16),
             slots,
@@ -562,19 +567,18 @@
             slots,
             pltpu.VMEM((6, VOCAB_DEV, THIRD_PAD), F32),
             pltpu.VMEM((3, THIRD_PAD, PACKS * PACK_ROWS), BF16),
-            pltpu.VMEM((PACKS * PACK_ROWS, LANES), BF16),
             pltpu.VMEM((PACKS, PACK_ROWS, LANES), BF16),
             pltpu.VMEM((2, PACK_ROWS, 4 * LANES), BF16),
             pltpu.VMEM((2, BLOCKS, LANES), F32),
             pltpu.VMEM((2, PACKS, LANES), jnp.int32),
             pltpu.VMEM((2 * PACKS, 1, LANES), F32),
-            pltpu.VMEM((PACKS, 1, LANES), F32),
+            pltpu.VMEM((2 * PACKS, 1, LANES), F32),
             pltpu.VMEM((2, 1, LANES), F32),
             pltpu.VMEM((2, 1, LANES), F32),
-            pltpu.VMEM((PACKS, 8, LANES), F32),
-            pltpu.VMEM((PACKS, 8, LANES), F32),
-            pltpu.VMEM((8, LANES), F32),
-            pltpu.VMEM((PACKS, 8, LANES), F32),
+            pltpu.VMEM((3, PACKS * PACK_ROWS, LANES), BF16),
+            pltpu.VMEM((6, THIRD_PAD, LANES), F32),
+            pltpu.VMEM((PACKS, 4, LANES), F32),
+            pltpu.VMEM((PACKS * PACKS, 4, LANES), F32),
             pltpu.VMEM((3, 8, THIRD_PAD), jnp.int32),
             dma((6,)),
             dma((2,)),
@@ -583,15 +587,12 @@
             dma,
             dma((16,)),
             dma((16,)),
-            dma((8,)),
-            dma((8,)),
-            dma,
+            dma((16,)),
+            dma((16,)),
             dma((3,)),
             dma((192,)),
-            dma((8,)),
-            dma((8,)),
-            dma((8,)),
-            dma((8,)),
+            dma,
+            dma,
         ],
         compiler_params=pltpu.CompilerParams(
             collective_id=0, has_side_effects=True, vmem_limit_bytes=60 * 1024 * 1024
@@ -609,8 +610,15 @@
         dom_gain.reshape(BLOCKS, LANES),
         dom_head,
         targets.reshape(PACKS, LANES),
-        doc_ids.reshape(PACKS, LANES),
+        docs,
     )
+    token, score = pl.pallas_call(
+        finish,
+        out_shape=(
+            jax.ShapeDtypeStruct((1, PACK_ROWS), F32),
+            jax.ShapeDtypeStruct((1, DOC_PACK), F32),
+        ),
+    )(total, docs)
     return token.reshape(PACK_ROWS), score.reshape(DOC_PACK)
 
 

time: 100 us -> 79.1 us (0.79)
  Pallas kernels: 97 us -> 78.3 us
  local copies, waits for them, and re-layouts: 2.25 us -> 0 us
    pallas_call x1 -> x2, Pallas kernels: 97 us -> 78.3 us  [the longest x1 77 us: per_device(): pl.pallas_call(kernel, out_shape=jax.ShapeDtypeStruct((4, LANES), F32), i...]
    unnamed x2 -> x0, local copies, waits for them, and re-layouts: 2.25 us -> none
where the time goes in v2:
time: 79.1 us; the launch traced here: 79 us
  Pallas kernels  78.3 us (99%)
    pallas_call x1, Pallas kernels, per_device(): pl.pallas_call(kernel, out_shape=jax.ShapeDtypeStruct((4, LANES), F32), i...  77 us

profile of v2, /device:TPU:0, one launch (start us, length us, event | category | flops | bytes accessed | tf_op | source)
XLA Modules:
  0.0 79.0 jit_solution(17329182259287909435)
XLA Ops:
  0.6 77.0 %shard_map.95.total = f32[4,128]{1,0:T(4,128)} custom-call(bf16[128,512]{1,0:T(8,128)(2,1)} %gen_hidden.1, f32[32,128]{1,0:T(8,128)} %bitcast.8, bf16[1024,4096]{1,0:T(8,128)(2,1)} %gen_head.1, bf16[128,512]{1,0:T(8,128)(2,1)} %dom_hidden.1, f32[32,128]{1,0:T(8,128)} %bitcast.9, bf16[1024,4096]{1,0:T(8,128)(2,1)} %dom_head.1, s32[8,128]{1,0:T(8,128)} %bitcast.10, ...), custom_call_target="tpu_custom_call" | custom-call | flops 9126805504 | bytes 16777216 | tf_op jit(solution)/shard_map/pallas_call | solution.py:558
  77.7 1.3 %shard_map.96 = (f32[1,128]{1,0:T(1,128)}, f32[1,8]{1,0:T(1,128)}) custom-call(f32[4,128]{1,0:T(4,128)} %shard_map.95.total, s32[8,128]{1,0:T(8,128)} %bitcast.7), custom_call_target="tpu_custom_call" | custom-call | tf_op jit(solution)/shard_map/pallas_call | solution.py:615

commit v3 on v2

--- a/solution.py
+++ b/solution.py
@@ -25,6 +25,21 @@
 
 def turn(q):
     return q + q // 2 - 2 * (q // 3)
+
+
+LAYER_HALF = (0, 0, 1, 0, 1, 1, 0, 1)
+LAYER_LAST = (0, 3, 0, 1, 3, 1, 2, 2)
+CHUNKS = ((0, 1), (1, 3), (4, 4), (8, 4), (12, 4))
+SENT_AT = {3: 0, 4: 1}
+RELAYED_AT = (0, 0, 2, 3, 4)
+
+
+def pick(table, k):
+    value = jnp.int32(table[0])
+    for i in range(1, len(table)):
+        if table[i] != table[i - 1]:
+            value = jnp.where(k >= i, jnp.int32(table[i]), value)
+    return value
 
 
 def device_of(x, y, z):
@@ -77,6 +92,7 @@
     stats_src,
     stats_in,
     want,
+    target_parts,
     load_sem,
     head_sem,
     stage_send,
@@ -97,7 +113,6 @@
     sign = 1 - 2 * core
     x, y, z = g % 4, (g // 4) * 2 + d % 2, d // 2
     here = (x, y, z)
-    own_slot = slot_of(x, y, z)
     is_dom = (x + y) % 2
 
     barrier = pltpu.get_barrier_semaphore()
@@ -126,6 +141,37 @@
     for load in loads:
         load.start()
 
+    pl.semaphore_wait(barrier, 2 * (PACKS - 1) + 1)
+
+    gen_targets = [2 * q + g % 2 for q in range(4)]
+    dom_targets = [2 * q + (d + 1) % 2 for q in range(4)]
+
+    def stage_copy(q, model):
+        cols = pl.ds(q * LANES, LANES)
+        if model == 0:
+            src, row, device = gen_hidden.at[:, cols], d, {"dom": gen_targets[q]}
+        else:
+            src, row, device = dom_hidden.at[:, cols], g, {"gen": dom_targets[q]}
+        far = remote(
+            src, stage.at[row], stage_send.at[model * 4 + q], stage_recv.at[row], device
+        )
+        near = pltpu.make_async_copy(src, stage.at[row], local_sem)
+        return far, near
+
+    def targets_self(q, model):
+        return gen_targets[q] == d if model == 0 else dom_targets[q] == g
+
+    def each_stage(act_far, act_near):
+        for model in range(2):
+            for q in range(4):
+                mine = targets_self(q, model)
+                far, near = stage_copy(q, model)
+                if act_near is not None:
+                    pl.when(mine)(lambda near=near: act_near(near))
+                pl.when(jnp.logical_not(mine))(lambda far=far: act_far(far))
+
+    each_stage(lambda c: c.start(), lambda c: c.start())
+
     loads[0].wait()
     loads[1].wait()
     for model in range(2):
@@ -139,37 +185,6 @@
             square_in[pl.ds(g, 1)] = row[None]
         else:
             square_in[pl.ds(PACKS + d, 1)] = row[None]
-
-    pl.semaphore_wait(barrier, 2 * (PACKS - 1) + 1)
-
-    gen_targets = [2 * q + g % 2 for q in range(4)]
-    dom_targets = [2 * q + (d + 1) % 2 for q in range(4)]
-
-    def stage_copy(q, model):
-        cols = pl.ds(q * LANES, LANES)
-        if model == 0:
-            src, row, device = gen_hidden.at[:, cols], d, {"dom": gen_targets[q]}
-        else:
-            src, row, device = dom_hidden.at[:, cols], g, {"gen": dom_targets[q]}
-        far = remote(
-            src, stage.at[row], stage_send.at[model * 4 + q], stage_recv.at[row], device
-        )
-        near = pltpu.make_async_copy(src, stage.at[row], local_sem)
-        return far, near
-
-    def targets_self(q, model):
-        return gen_targets[q] == d if model == 0 else dom_targets[q] == g
-
-    def each_stage(act_far, act_near):
-        for model in range(2):
-            for q in range(4):
-                mine = targets_self(q, model)
-                far, near = stage_copy(q, model)
-                if act_near is not None:
-                    pl.when(mine)(lambda near=near: act_near(near))
-                pl.when(jnp.logical_not(mine))(lambda far=far: act_far(far))
-
-    each_stage(lambda c: c.start(), lambda c: c.start())
 
     def square_copy(step, model):
         if model == 0:
@@ -190,39 +205,6 @@
         for model in range(2):
             square_copy(step, model)[0].start()
 
-    def load_heads(k, carry):
-        cols = pl.ds(pl.multiple_of(k * LANES, LANES), LANES)
-        pltpu.make_async_copy(gen_head.at[:, cols], heads.at[0, k], head_sem.at[0]).start()
-        pltpu.make_async_copy(dom_head.at[:, cols], heads.at[1, k], head_sem.at[1]).start()
-        return carry
-
-    lax.fori_loop(0, BLOCKS, load_heads, 0)
-
-    for step in range(1, PACKS):
-        for model in range(2):
-            square_copy(step, model)[1].wait_recv()
-    for model in range(2):
-        row = jnp.sum(square_in[model * PACKS : (model + 1) * PACKS], axis=0)
-        square_src_full[model] = row
-        own = d if model == 0 else PACKS + g
-        square_full[pl.ds(own, 1)] = row[None]
-
-    def full_copy(step, model):
-        back = PACKS - step
-        if model == 0:
-            device, own, other = {"dom": (d + step) % PACKS}, d, (d + back) % PACKS
-        else:
-            device = {"gen": (g + step) % PACKS}
-            own, other = PACKS + g, PACKS + (g + back) % PACKS
-        src, send = square_src_full.at[model], full_send.at[model * PACKS + step]
-        out = remote(src, square_full.at[own], send, full_recv.at[own], device)
-        arrival = remote(src, square_full.at[other], send, full_recv.at[other], device)
-        return out, arrival
-
-    for step in range(1, PACKS):
-        for model in range(2):
-            full_copy(step, model)[0].start()
-
     for load in loads[2:]:
         load.wait()
     docs = ids[1]
@@ -238,27 +220,127 @@
             place[t, :, p * LANES : (p + 1) * LANES] = jnp.where(hit, 1.0, 0.0).astype(BF16)
         offset = offset + count
 
-    first_column = (g * PACKS + d) * VOCAB_DEV
-    tgt = ids[0]
-    high, low = tgt // 256, tgt % 256
-    pieces = []
-    for t in range(3):
-        got = jnp.zeros((32, THIRD_PAD), F32)
-        for p in range(PACKS):
-            rows = lax.broadcasted_iota(jnp.int32, (32, LANES), 0)
-            pair = jnp.where(
-                rows < 16,
-                jnp.broadcast_to(high[p : p + 1, :], (32, LANES)),
-                jnp.broadcast_to(low[p : p + 1, :], (32, LANES)),
-            )
-            got = got + lax.dot_general(
-                pair.astype(F32).astype(BF16),
-                place[t, :, p * LANES : (p + 1) * LANES],
-                (((1,), (1,)), ((), ())),
-                preferred_element_type=F32,
-            )
-        column = (got[0:8] * 256.0 + got[16:24]).astype(jnp.int32) - first_column
-        want[t] = column
+    def source(p):
+        return jnp.where(is_dom == 1, g, d) == p
+
+    for p in range(PACKS):
+        mine = source(p)
+
+        @pl.when(jnp.logical_not(mine))
+        def _(p=p):
+            remote(
+                stage.at[p], stage.at[p], stage_send.at[0], stage_recv.at[p], {"dom": d}
+            ).wait_recv()
+
+        @pl.when(mine)
+        def _(p=p):
+            pltpu.make_async_copy(stage.at[p], stage.at[p], local_sem).wait()
+
+    for t in range(3):
+        rows = jnp.dot(
+            place[t],
+            stage[...].reshape(PACKS * PACK_ROWS, LANES),
+            preferred_element_type=F32,
+        ).astype(BF16)
+        thirds[t][0] = rows
+
+    def moved(axis, by):
+        at = list(here)
+        at[axis] = (at[axis] + by + 4) % 4
+        return device_of(*at)
+
+    ahead = [moved(axis, sign) for axis in range(3)]
+    behind = [moved(axis, -sign) for axis in range(3)]
+
+    def block_at(t, n, last):
+        at = list(here)
+        for k, u in enumerate((turn(n % 4), turn(n // 4), last)):
+            axis = AXES[t][k]
+            at[axis] = (at[axis] - sign * u + 4) % 4
+        return slot_of(*at)
+
+    def rows_of(t, slot, count):
+        return thirds[t].at[pl.ds(slot, count), pl.ds(0, THIRD_ROWS[t])]
+
+    def push(t, k, forward, src, dst, count=1):
+        device = (ahead if forward else behind)[AXES[t][k]]
+        remote(
+            rows_of(t, src, count),
+            rows_of(t, dst, count),
+            ring_send.at[t],
+            ring_recv.at[t * 64 + dst],
+            device,
+        ).start()
+
+    def arrived(t, dst, count=1):
+        ref = rows_of(t, dst, count)
+        remote(ref, ref, ring_send.at[t], ring_recv.at[t * 64 + dst], ahead[0]).wait_recv()
+
+    def push_second(t, n):
+        push(t, 1, True, n, 4 + n)
+        push(t, 1, False, n, 8 + n)
+
+    def announce(t, c):
+        first, count = CHUNKS[c]
+        push(t, 2, True, first, 16 + first, count)
+        push(t, 2, False, first, 48 + first, count)
+
+    def relay(t, c):
+        first, count = CHUNKS[c]
+        arrived(t, 16 + first, count)
+        push(t, 2, True, 16 + first, 32 + first, count)
+
+    for t in range(3):
+        push(t, 0, True, 0, 1)
+        push(t, 0, False, 0, 2)
+    for t in range(3):
+        push_second(t, 0)
+    for t in range(3):
+        announce(t, 0)
+
+    def load_heads(k, carry):
+        cols = pl.ds(pl.multiple_of(k * LANES, LANES), LANES)
+        pltpu.make_async_copy(gen_head.at[:, cols], heads.at[0, k], head_sem.at[0]).start()
+        pltpu.make_async_copy(dom_head.at[:, cols], heads.at[1, k], head_sem.at[1]).start()
+        return carry
+
+    lax.fori_loop(0, BLOCKS, load_heads, 0)
+
+    def first_axis(n):
+        for t in range(3):
+            arrived(t, n)
+            if n == 1:
+                push(t, 0, True, 1, 3)
+            push_second(t, n)
+
+    first_axis(1)
+
+    for step in range(1, PACKS):
+        for model in range(2):
+            square_copy(step, model)[1].wait_recv()
+    for model in range(2):
+        row = jnp.sum(square_in[model * PACKS : (model + 1) * PACKS], axis=0)
+        square_src_full[model] = row
+        own = d if model == 0 else PACKS + g
+        square_full[pl.ds(own, 1)] = row[None]
+
+    def full_copy(step, model):
+        back = PACKS - step
+        if model == 0:
+            device, own, other = {"dom": (d + step) % PACKS}, d, (d + back) % PACKS
+        else:
+            device = {"gen": (g + step) % PACKS}
+            own, other = PACKS + g, PACKS + (g + back) % PACKS
+        src, send = square_src_full.at[model], full_send.at[model * PACKS + step]
+        out = remote(src, square_full.at[own], send, full_recv.at[own], device)
+        arrival = remote(src, square_full.at[other], send, full_recv.at[other], device)
+        return out, arrival
+
+    for step in range(1, PACKS):
+        for model in range(2):
+            full_copy(step, model)[0].start()
+
+    first_axis(2)
 
     def clear(slot, carry):
         for t in range(3):
@@ -276,66 +358,61 @@
 
     lax.fori_loop(0, VOCAB_DEV // 64, clear_logits, 0)
 
-    def source(p):
-        return jnp.where(is_dom == 1, g, d) == p
-
+    first_axis(3)
+    for t in range(3):
+        announce(t, 1)
+
+    first_column = (g * PACKS + d) * VOCAB_DEV
+    tgt = ids[0]
+    high, low = tgt // 256, tgt % 256
+    rows = lax.broadcasted_iota(jnp.int32, (32, LANES), 0)
     for p in range(PACKS):
-        mine = source(p)
-
-        @pl.when(jnp.logical_not(mine))
-        def _(p=p):
-            remote(
-                stage.at[p], stage.at[p], stage_send.at[0], stage_recv.at[p], {"dom": d}
-            ).wait_recv()
-
-        @pl.when(mine)
-        def _(p=p):
-            pltpu.make_async_copy(stage.at[p], stage.at[p], local_sem).wait()
-
-    for t in range(3):
-        rows = jnp.dot(
-            place[t],
-            stage[...].reshape(PACKS * PACK_ROWS, LANES),
-            preferred_element_type=F32,
-        ).astype(BF16)
-        thirds[t][pl.ds(own_slot, 1)] = rows[None]
-
-    def moved(axis, by):
-        at = list(here)
-        at[axis] = (at[axis] + by + 4) % 4
-        return device_of(*at)
-
-    ahead = [moved(axis, sign) for axis in range(3)]
-    behind = [moved(axis, -sign) for axis in range(3)]
-
-    def slot_at(t, u):
-        at = list(here)
-        for k in range(3):
-            axis = AXES[t][k]
-            at[axis] = (at[axis] - sign * u[k] + 4) % 4
-        return slot_of(*at)
-
-    def piece(t, u):
-        return thirds[t].at[slot_at(t, u), pl.ds(0, THIRD_ROWS[t])]
-
-    def ring_index(t, u):
-        return t * 64 + u[0] * 16 + u[1] * 4 + u[2]
-
-    def push(t, u, k, forward):
-        new = list(u)
-        new[k] = new[k] + 1 if forward else 3
-        device = (ahead if forward else behind)[AXES[t][k]]
-        ref = piece(t, u)
-        remote(ref, ref, ring_send.at[t], ring_recv.at[ring_index(t, new)], device).start()
-
-    def arrived(t, u):
-        ref = piece(t, u)
-        remote(ref, ref, ring_send.at[t], ring_recv.at[ring_index(t, u)], ahead[0]).wait_recv()
-
-    for k in range(3):
+        pair = jnp.where(
+            rows < 16,
+            jnp.broadcast_to(high[p : p + 1, :], (32, LANES)),
+            jnp.broadcast_to(low[p : p + 1, :], (32, LANES)),
+        )
+        target_parts[:, p * LANES : (p + 1) * LANES] = pair.astype(F32).astype(BF16)
+    for t in range(3):
+        got = lax.dot_general(
+            target_parts[...], place[t], (((1,), (1,)), ((), ())), preferred_element_type=F32
+        )
+        column = (got[0:8] * 256.0 + got[16:24]).astype(jnp.int32) - first_column
+        want[t] = column
+
+    for n in range(4):
         for t in range(3):
-            push(t, (0, 0, 0), k, True)
-            push(t, (0, 0, 0), k, False)
+            arrived(t, 4 + n)
+            push(t, 1, True, 4 + n, 12 + n)
+    for t in range(3):
+        announce(t, 2)
+
+    def add_layer(t, half, last):
+        slots = [last * 16 + 8 * half + i for i in range(8)]
+        blocks = [block_at(t, 8 * half + i, last) for i in range(8)]
+        if t == 0:
+            order = (0, 3, 5, 6, 1, 2, 4, 7)
+        elif t == 1:
+            order = (0, 3, 4, 7, 1, 2, 5, 6)
+        else:
+            order = (0, 1, 2, 3, 4, 5, 6, 7)
+        for group in (order[:4], order[4:]):
+            model = blocks[group[0]] // BLOCKS
+            part = [blocks[i] % BLOCKS for i in group]
+            left = jnp.concatenate([heads[model, b] for b in part], axis=1)
+            scale = scales[2 * t + model]
+            right = jnp.concatenate(
+                [
+                    (
+                        thirds[t][slots[i]].astype(F32) * scale * gains[model, pl.ds(b, 1), :]
+                    ).astype(BF16)
+                    for i, b in zip(group, part)
+                ],
+                axis=1,
+            )
+            logits[2 * t + model] += lax.dot_general(
+                left, right, (((1,), (1,)), ((), ())), preferred_element_type=F32
+            )
 
     for step in range(1, PACKS):
         for model in range(2):
@@ -356,95 +433,31 @@
                 )
             scales[2 * t + model] = total
 
-    for first in (1, 3, 2):
-        for t in range(3):
-            u = (first, 0, 0)
-            arrived(t, u)
-            if first == 1:
-                push(t, u, 0, True)
-            push(t, u, 1, True)
-            push(t, u, 1, False)
-    for first in (1, 3, 2):
-        for t in range(3):
-            push(t, (first, 0, 0), 2, True)
-            push(t, (first, 0, 0), 2, False)
-
-    def line(n, last):
-        return turn(n % 4), turn(n // 4), last
-
-    def announce(t, n):
-        push(t, line(n, 0), 2, True)
-        push(t, line(n, 0), 2, False)
-
-    def relay(t, n):
-        arrived(t, line(n, 1))
-        push(t, line(n, 1), 2, True)
-
-    def middle(i, carry):
-        for t in range(3):
-            u = (turn(i), 1, 0)
-            arrived(t, u)
-            push(t, u, 1, True)
-            push(t, u, 2, True)
-            push(t, u, 2, False)
-        return carry
-
-    lax.fori_loop(0, 4, middle, 0)
-
-    def add_layer(t, half, last):
-        slots = [slot_at(t, line(8 * half + i, last)) for i in range(8)]
-        if t == 0:
-            order = (0, 3, 5, 6, 1, 2, 4, 7)
-        elif t == 1:
-            order = (0, 3, 4, 7, 1, 2, 5, 6)
-        else:
-            order = (0, 1, 2, 3, 4, 5, 6, 7)
-        for group in (order[:4], order[4:]):
-            group = [slots[i] for i in group]
-            model = group[0] // BLOCKS
-            left = jnp.concatenate([heads[model, s % BLOCKS] for s in group], axis=1)
-            scale = scales[2 * t + model]
-            right = jnp.concatenate(
-                [
-                    (
-                        thirds[t][s].astype(F32) * scale * gains[model, pl.ds(s % BLOCKS, 1), :]
-                    ).astype(BF16)
-                    for s in group
-                ],
-                axis=1,
-            )
-            logits[2 * t + model] += lax.dot_general(
-                left, right, (((1,), (1,)), ((), ())), preferred_element_type=F32
-            )
-
     pltpu.make_async_copy(heads.at[0], heads.at[0], head_sem.at[0]).wait()
     pltpu.make_async_copy(heads.at[1], heads.at[1], head_sem.at[1]).wait()
 
     def layer(k, carry):
-        half = jnp.where((k == 3) | (k >= 5), 1, 0)
-        last = jnp.where((k == 1) | (k == 5), 3, 0)
-        last = jnp.where((k == 2) | (k == 6), 1, last)
-        last = jnp.where((k == 4) | (k == 7), 2, last)
+        half, last = pick(LAYER_HALF, k), pick(LAYER_LAST, k)
         for t in range(3):
 
-            @pl.when(last >= 2)
-            def _(t=t):
-                for i in range(8):
-                    arrived(t, line(8 * half + i, last))
+            for c in (3, 4):
+
+                @pl.when(k == SENT_AT[c])
+                def _(t=t, c=c):
+                    for n in range(CHUNKS[c][0], CHUNKS[c][0] + CHUNKS[c][1]):
+                        arrived(t, n)
+                    announce(t, c)
+
+            for c in range(5):
+                pl.when(k == RELAYED_AT[c])(lambda t=t, c=c: relay(t, c))
+            for h, held in enumerate(((0, 1, 2), (3, 4))):
+
+                @pl.when((last >= 2) & (half == h))
+                def _(t=t, held=held):
+                    for c in held:
+                        arrived(t, last * 16 + CHUNKS[c][0], CHUNKS[c][1])
 
             add_layer(t, half, last)
-
-            @pl.when(k < 2)
-            def _(t=t):
-                for i in range(4):
-                    n = 8 + 4 * k + i
-                    arrived(t, line(n, 0))
-                    announce(t, n)
-
-            @pl.when((k < 2) | (k == 3) | (k == 4))
-            def _(t=t):
-                for i in range(4):
-                    relay(t, 4 * (k - k // 3) + i)
 
         return carry
 
@@ -580,6 +593,7 @@
             pltpu.VMEM((PACKS, 4, LANES), F32),
             pltpu.VMEM((PACKS * PACKS, 4, LANES), F32),
             pltpu.VMEM((3, 8, THIRD_PAD), jnp.int32),
+            pltpu.VMEM((32, PACKS * PACK_ROWS), BF16),
             dma((6,)),
             dma((2,)),
             dma((8,)),

time: 79.1 us -> 73.8 us (0.933)
  Pallas kernels: 78.3 us -> 72.9 us
    pallas_call x1, Pallas kernels: 77 us -> 71.6 us  [per_device(): pl.pallas_call(kernel, out_shape=jax.ShapeDtypeStruct((4, LANES), F32), i...]
where the time goes in v3:
time: 73.8 us; the launch traced here: 73.6 us
  Pallas kernels  72.9 us (99%)
    pallas_call x1, Pallas kernels, per_device(): pl.pallas_call(kernel, out_shape=jax.ShapeDtypeStruct((4, LANES), F32), i...  71.6 us

profile of v3, /device:TPU:0, one launch (start us, length us, event | category | flops | bytes accessed | tf_op | source)
XLA Modules:
  0.0 73.6 jit_solution(8688780536020936958)
XLA Ops:
  0.6 71.6 %shard_map.95.total = f32[4,128]{1,0:T(4,128)} custom-call(bf16[128,512]{1,0:T(8,128)(2,1)} %gen_hidden.1, f32[32,128]{1,0:T(8,128)} %bitcast.8, bf16[1024,4096]{1,0:T(8,128)(2,1)} %gen_head.1, bf16[128,512]{1,0:T(8,128)(2,1)} %dom_hidden.1, f32[32,128]{1,0:T(8,128)} %bitcast.9, bf16[1024,4096]{1,0:T(8,128)(2,1)} %dom_head.1, s32[8,128]{1,0:T(8,128)} %bitcast.10, ...), custom_call_target="tpu_custom_call" | custom-call | flops 9126805504 | bytes 16777216 | tf_op jit(solution)/shard_map/pallas_call | solution.py:571
  72.3 1.3 %shard_map.96 = (f32[1,128]{1,0:T(1,128)}, f32[1,8]{1,0:T(1,128)}) custom-call(f32[4,128]{1,0:T(4,128)} %shard_map.95.total, s32[8,128]{1,0:T(8,128)} %bitcast.7), custom_call_target="tpu_custom_call" | custom-call | tf_op jit(solution)/shard_map/pallas_call | solution.py:629

commit v4 on v3

--- a/solution.py
+++ b/solution.py
@@ -31,7 +31,7 @@
 LAYER_LAST = (0, 3, 0, 1, 3, 1, 2, 2)
 CHUNKS = ((0, 1), (1, 3), (4, 4), (8, 4), (12, 4))
 SENT_AT = {3: 0, 4: 1}
-RELAYED_AT = (0, 0, 2, 3, 4)
+RELAYED_AT = (0, 1, 2, 3, 4)
 
 
 def pick(table, k):
@@ -220,6 +220,14 @@
             place[t, :, p * LANES : (p + 1) * LANES] = jnp.where(hit, 1.0, 0.0).astype(BF16)
         offset = offset + count
 
+    def load_heads(k, carry):
+        cols = pl.ds(pl.multiple_of(k * LANES, LANES), LANES)
+        pltpu.make_async_copy(gen_head.at[:, cols], heads.at[0, k], head_sem.at[0]).start()
+        pltpu.make_async_copy(dom_head.at[:, cols], heads.at[1, k], head_sem.at[1]).start()
+        return carry
+
+    lax.fori_loop(0, BLOCKS, load_heads, 0)
+
     def source(p):
         return jnp.where(is_dom == 1, g, d) == p
 
@@ -297,14 +305,6 @@
         push_second(t, 0)
     for t in range(3):
         announce(t, 0)
-
-    def load_heads(k, carry):
-        cols = pl.ds(pl.multiple_of(k * LANES, LANES), LANES)
-        pltpu.make_async_copy(gen_head.at[:, cols], heads.at[0, k], head_sem.at[0]).start()
-        pltpu.make_async_copy(dom_head.at[:, cols], heads.at[1, k], head_sem.at[1]).start()
-        return carry
-
-    lax.fori_loop(0, BLOCKS, load_heads, 0)
 
     def first_axis(n):
         for t in range(3):
@@ -463,7 +463,7 @@
 
     lax.fori_loop(0, 8, layer, 0)
 
-    CHUNK = 64
+    CHUNK = 128
     steps = VOCAB_DEV // CHUNK
     spread = jnp.zeros((32, VOCAB_DEV), F32)
     for t in range(3):

time: 73.8 us -> 73.5 us (level)
  no operation moved by 1% of the time
where the time goes in v4:
time: 73.5 us; the launch traced here: 73.3 us
  Pallas kernels  72.7 us (99%)
    pallas_call x1, Pallas kernels, per_device(): pl.pallas_call(kernel, out_shape=jax.ShapeDtypeStruct((4, LANES), F32), i...  71.4 us

profile of v4, /device:TPU:0, one launch (start us, length us, event | category | flops | bytes accessed | tf_op | source)
XLA Modules:
  0.0 73.3 jit_solution(8108118873083988859)
XLA Ops:
  0.6 71.4 %shard_map.95.total = f32[4,128]{1,0:T(4,128)} custom-call(bf16[128,512]{1,0:T(8,128)(2,1)} %gen_hidden.1, f32[32,128]{1,0:T(8,128)} %bitcast.8, bf16[1024,4096]{1,0:T(8,128)(2,1)} %gen_head.1, bf16[128,512]{1,0:T(8,128)(2,1)} %dom_hidden.1, f32[32,128]{1,0:T(8,128)} %bitcast.9, bf16[1024,4096]{1,0:T(8,128)(2,1)} %dom_head.1, s32[8,128]{1,0:T(8,128)} %bitcast.10, ...), custom_call_target="tpu_custom_call" | custom-call | flops 9126805504 | bytes 16777216 | tf_op jit(solution)/shard_map/pallas_call | solution.py:571
  72.0 1.3 %shard_map.96 = (f32[1,128]{1,0:T(1,128)}, f32[1,8]{1,0:T(1,128)}) custom-call(f32[4,128]{1,0:T(4,128)} %shard_map.95.total, s32[8,128]{1,0:T(8,128)} %bitcast.7), custom_call_target="tpu_custom_call" | custom-call | tf_op jit(solution)/shard_map/pallas_call | solution.py:629
